TPU v7x, 32 devices: a whole 2x2x4 slice. The times are simulated.
32 devices in a mesh: rows: 4 (over z), cols: 8 (over y, x, core).
Axes of the slice: x: 2, y: 2, z: 4, core: 2. Of those that a mesh axis runs over, the one named last changes fastest.
Arguments:
- tokens: bfloat16 [32, 1024, 768], P('rows', 'cols'), may hold values from -6 to 6
- segment_ids: int32 [32, 1024], P('rows'), may hold values from 0 to 3, never falling along the last dimension, each value on 1 to 768 neighbouring positions
- cotangent: bfloat16 [32, 1024, 768], P('rows', 'cols'), may hold values from -6 to 6
- w_qkv: bfloat16 [768, 2304], replicated, may hold values from -0.21875 to 0.21875
- q_bias: float32 [768], replicated, may hold values from -1.2 to 1.2
- v_bias: float32 [768], replicated, may hold values from -1.2 to 1.2
- w_out: bfloat16 [768, 768], replicated, may hold values from -1.75 to 1.75
- out_bias: float32 [768], replicated, may hold values from -1.2 to 1.2
- attn_gain: float32 [768], replicated, may hold values from 0.5 to 1.5
- attn_shift: float32 [768], replicated, may hold values from -1.2 to 1.2
- mlp_gain: float32 [768], replicated, may hold values from 0.5 to 1.5
- mlp_shift: float32 [768], replicated, may hold values from -1.2 to 1.2
- w_up: bfloat16 [768, 3072], replicated, may hold values from -0.21875 to 0.21875
- up_bias: float32 [3072], replicated, may hold values from -1.2 to 1.2
- w_down: bfloat16 [3072, 768], replicated, may hold values from -0.109375 to 0.109375
- down_bias: float32 [768], replicated, may hold values from -1.2 to 1.2
Outputs:
- output: bfloat16 [32, 1024, 768], P('rows', 'cols')
- grad_tokens: float32 [32, 1024, 768], P('rows', 'cols')
- grad_w_qkv: float32 [768, 2304], replicated
- grad_q_bias: float32 [768], replicated
- grad_v_bias: float32 [768], replicated
- grad_w_out: float32 [768, 768], replicated
- grad_out_bias: float32 [768], replicated
- grad_attn_gain: float32 [768], replicated
- grad_attn_shift: float32 [768], replicated
- grad_mlp_gain: float32 [768], replicated
- grad_mlp_shift: float32 [768], replicated
- grad_w_up: float32 [768, 3072], replicated
- grad_up_bias: float32 [3072], replicated
- grad_w_down: float32 [3072, 768], replicated
- grad_down_bias: float32 [768], replicated
Inputs may be any that keep to these rules, and one draw needn't show every extreme that they name: `segment_ids`: along each stored sequence the ids never fall; each document is a run of slots.
All inputs are finite; a program needn't handle non-finite values.
Results may differ from a plain program's by a relative error of at most 0.012.
Values may be sent and summed in bfloat16 or wider, within the bound.
A program may use at most 384 MiB of HBM per device.

v0:
```python
import jax
import jax.numpy as jnp
from jax import lax
from jax.sharding import PartitionSpec as P

HEADS = 12
HDIM = 64
LEN = 1024


def combined_all(value, axis, combine):
    everything = jax.tree.map(lambda part: lax.all_gather(part, axis), value)
    first = jax.tree.map(lambda part: part[0], everything)

    def turn(k, so_far):
        return combine(so_far, jax.tree.map(lambda part: part[k], everything))

    return lax.fori_loop(1, lax.axis_size(axis), turn, first)


def norm_rows(values, gain_vec, shift_vec):
    average = jnp.mean(values, axis=-1, keepdims=True)
    centered = values - average
    variance = jnp.mean(centered * centered, axis=-1, keepdims=True)
    return centered * lax.rsqrt(variance + 1e-05) * gain_vec + shift_vec


def gelu_tanh(values):
    return jax.nn.gelu(values, approximate=True)


def merge_stats(former, latter):
    row_peak = jnp.maximum(former[0], latter[0])
    row_total = former[1] * jnp.exp(former[0] - row_peak) + latter[1] * jnp.exp(
        latter[0] - row_peak
    )
    return (row_peak, row_total)


def split_heads(values):
    return values.reshape(values.shape[0], values.shape[1], HEADS, HDIM)


def score_parts(queries_all, keys_local, segment_ids, column):
    seq_count, length, model_width = queries_all.shape
    key_count = keys_local.shape[1]
    scores = jnp.einsum(
        "sjhd,sihd->shji",
        split_heads(keys_local),
        split_heads(queries_all),
        preferred_element_type=jnp.float32,
    ) * HDIM ** (-0.5)
    key_first = column * key_count
    key_pos = key_first + jnp.arange(key_count, dtype=jnp.int32)
    query_pos = jnp.arange(length, dtype=jnp.int32)
    row_starts = jnp.concatenate(
        [segment_ids[:, :-1] != segment_ids[:, 1:], jnp.ones((seq_count, 1), dtype=bool)], axis=1
    )
    key_starts = lax.dynamic_slice_in_dim(row_starts, key_first, key_count, 1)
    key_segs = lax.dynamic_slice_in_dim(segment_ids, key_first, key_count, 1)
    same_doc = key_segs[:, :, None] == segment_ids[:, None, :]
    allowed = same_doc & (query_pos[None, None, :] <= key_pos[None, :, None])
    picked = (
        same_doc
        & (query_pos[None, None, :] < key_pos[None, :, None])
        & jnp.logical_not(key_starts)[:, :, None]
    )
    selected = jnp.where(picked, jax.nn.relu(scores[:, 0]), 0.0)
    carried = lax.cumsum(selected, axis=2, reverse=True) - selected
    logits = jnp.where(allowed[:, None], scores - 8.0 / LEN * carried[:, None], -1e30)
    return (scores, logits, allowed, picked)


def per_device(
    tokens,
    segment_ids,
    cotangent,
    w_qkv,
    q_bias,
    v_bias,
    w_out,
    out_bias,
    attn_gain,
    attn_shift,
    mlp_gain,
    mlp_shift,
    w_up,
    up_bias,
    w_down,
    down_bias,
):
    seq_count, key_count, model_width = tokens.shape
    column = lax.axis_index("cols")
    inputs = tokens.astype(jnp.float32).reshape(-1, model_width)
    normed_low = norm_rows(inputs, attn_gain, attn_shift).astype(jnp.bfloat16)
    projected = jnp.dot(normed_low, w_qkv, preferred_element_type=jnp.float32)
    queries = (
        (projected[:, :model_width] + q_bias)
        .astype(jnp.bfloat16)
        .reshape(seq_count, key_count, model_width)
    )
    keys_local = (
        projected[:, model_width : 2 * model_width]
        .astype(jnp.bfloat16)
        .reshape(seq_count, key_count, model_width)
    )
    values_local = (
        (projected[:, 2 * model_width :] + v_bias)
        .astype(jnp.bfloat16)
        .reshape(seq_count, key_count, model_width)
    )
    queries_all = lax.all_gather(queries, "cols", axis=1, tiled=True)
    length = queries_all.shape[1]
    scores, logits, allowed, picked = score_parts(queries_all, keys_local, segment_ids, column)
    local_peak = jnp.max(logits, axis=2)
    local_total = jnp.sum(
        jnp.where(allowed[:, None], jnp.exp(logits - local_peak[:, :, None, :]), 0.0), axis=2
    )
    row_peak, row_total = combined_all((local_peak, local_total), "cols", merge_stats)
    probs_low = jnp.where(
        allowed[:, None], jnp.exp(logits - row_peak[:, :, None, :]) / row_total[:, :, None, :], 0.0
    ).astype(jnp.bfloat16)
    partial_out = jnp.einsum(
        "shji,sjhd->sihd", probs_low, split_heads(values_local), preferred_element_type=jnp.float32
    ).reshape(seq_count, length, model_width)
    attended = lax.psum_scatter(partial_out, "cols", scatter_dimension=1, tiled=True)
    attended_low = attended.astype(jnp.bfloat16).reshape(-1, model_width)
    residual = inputs + jnp.dot(attended_low, w_out, preferred_element_type=jnp.float32) + out_bias
    normed_two = norm_rows(residual, mlp_gain, mlp_shift).astype(jnp.bfloat16)
    upper = jnp.dot(normed_two, w_up, preferred_element_type=jnp.float32) + up_bias
    act_low = gelu_tanh(upper).astype(jnp.bfloat16)
    final_sum = residual + jnp.dot(act_low, w_down, preferred_element_type=jnp.float32) + down_bias
    output = final_sum.astype(jnp.bfloat16).reshape(seq_count, key_count, model_width)
    grad_out = cotangent.reshape(-1, model_width)
    grad_top = grad_out.astype(jnp.float32)
    g_down_bias = jnp.sum(grad_top, axis=0)
    g_w_down = jnp.dot(act_low.T, grad_out, preferred_element_type=jnp.float32)
    grad_act = jnp.dot(grad_out, w_down.T, preferred_element_type=jnp.float32)
    gelu_value, gelu_back = jax.vjp(gelu_tanh, upper)
    grad_upper = gelu_back(grad_act)[0].astype(jnp.bfloat16)
    g_up_bias = jnp.sum(grad_upper.astype(jnp.float32), axis=0)
    g_w_up = jnp.dot(normed_two.T, grad_upper, preferred_element_type=jnp.float32)
    grad_normed_two = jnp.dot(grad_upper, w_up.T, preferred_element_type=jnp.float32)
    norm_value, second_back = jax.vjp(norm_rows, residual, mlp_gain, mlp_shift)
    grad_res_part, g_mlp_gain, g_mlp_shift = second_back(grad_normed_two)
    grad_residual = grad_top + grad_res_part
    grad_branch = grad_residual.astype(jnp.bfloat16)
    g_out_bias = jnp.sum(grad_branch.astype(jnp.float32), axis=0)
    g_w_out = jnp.dot(attended_low.T, grad_branch, preferred_element_type=jnp.float32)
    grad_attended = (
        jnp.dot(grad_branch, w_out.T, preferred_element_type=jnp.float32)
        .astype(jnp.bfloat16)
        .reshape(seq_count, key_count, model_width)
    )
    block_sums = lax.psum(
        (g_w_out, g_out_bias, g_mlp_gain, g_mlp_shift, g_w_up, g_up_bias, g_w_down, g_down_bias),
        ("rows", "cols"),
    )
    grad_out_all = lax.all_gather(grad_attended, "cols", axis=1, tiled=True)
    scores, logits, allowed, picked = score_parts(queries_all, keys_local, segment_ids, column)
    probs_full = jnp.where(
        allowed[:, None], jnp.exp(logits - row_peak[:, :, None, :]) / row_total[:, :, None, :], 0.0
    )
    probs_back = probs_full.astype(jnp.bfloat16)
    grad_heads = split_heads(grad_out_all)
    grad_probs = jnp.einsum(
        "sihd,sjhd->shji", grad_heads, split_heads(values_local), preferred_element_type=jnp.float32
    )
    local_delta = jnp.sum(probs_full * grad_probs, axis=2)
    delta = lax.psum(local_delta, "cols")
    grad_logits = probs_full * (grad_probs - delta[:, :, None, :])
    grad_carried = -(8.0 / LEN) * jnp.sum(grad_logits, axis=1)
    grad_selected = lax.cumsum(grad_carried, axis=2) - grad_carried
    grad_head_zero = jnp.where(picked & (scores[:, 0] > 0), grad_selected, 0.0)
    grad_scores = jnp.concatenate(
        [grad_logits[:, :1] + grad_head_zero[:, None], grad_logits[:, 1:]], axis=1
    ).astype(jnp.bfloat16)
    grad_q_part = (
        jnp.einsum(
            "shji,sjhd->sihd",
            grad_scores,
            split_heads(keys_local),
            preferred_element_type=jnp.float32,
        )
        * HDIM ** (-0.5)
    ).reshape(seq_count, length, model_width)
    grad_queries = (
        lax.psum_scatter(grad_q_part, "cols", scatter_dimension=1, tiled=True)
        .astype(jnp.bfloat16)
        .reshape(-1, model_width)
    )
    grad_keys = (
        (
            jnp.einsum(
                "shji,sihd->sjhd",
                grad_scores,
                split_heads(queries_all),
                preferred_element_type=jnp.float32,
            )
            * HDIM ** (-0.5)
        )
        .astype(jnp.bfloat16)
        .reshape(-1, model_width)
    )
    grad_values = (
        jnp.einsum("shji,sihd->sjhd", probs_back, grad_heads, preferred_element_type=jnp.float32)
        .astype(jnp.bfloat16)
        .reshape(-1, model_width)
    )
    grad_proj = jnp.concatenate([grad_queries, grad_keys, grad_values], axis=1)
    g_q_bias = jnp.sum(grad_queries.astype(jnp.float32), axis=0)
    g_v_bias = jnp.sum(grad_values.astype(jnp.float32), axis=0)
    g_w_qkv = jnp.dot(normed_low.T, grad_proj, preferred_element_type=jnp.float32)
    grad_normed_one = jnp.dot(grad_proj, w_qkv.T, preferred_element_type=jnp.float32)
    first_value, first_back = jax.vjp(norm_rows, inputs, attn_gain, attn_shift)
    grad_in_part, g_attn_gain, g_attn_shift = first_back(grad_normed_one)
    grad_tokens = (grad_residual + grad_in_part).reshape(seq_count, key_count, model_width)
    attn_sums = lax.psum((g_w_qkv, g_q_bias, g_v_bias, g_attn_gain, g_attn_shift), ("rows", "cols"))
    summed = (
        attn_sums[0],
        attn_sums[1],
        attn_sums[2],
        block_sums[0],
        block_sums[1],
        attn_sums[3],
        attn_sums[4],
        block_sums[2],
        block_sums[3],
        block_sums[4],
        block_sums[5],
        block_sums[6],
        block_sums[7],
    )
    return (
        output,
        grad_tokens,
        summed[0],
        summed[1],
        summed[2],
        summed[3],
        summed[4],
        summed[5],
        summed[6],
        summed[7],
        summed[8],
        summed[9],
        summed[10],
        summed[11],
        summed[12],
    )


def solution(mesh):
    placed = (
        P("rows", "cols", None),
        P("rows", None),
        P("rows", "cols", None),
        P(),
        P(),
        P(),
        P(),
        P(),
        P(),
        P(),
        P(),
        P(),
        P(),
        P(),
        P(),
        P(),
    )
    return jax.shard_map(
        per_device,
        mesh=mesh,
        in_specs=placed,
        out_specs=(
            P("rows", "cols", None),
            P("rows", "cols", None),
            P(),
            P(),
            P(),
            P(),
            P(),
            P(),
            P(),
            P(),
            P(),
            P(),
            P(),
            P(),
            P(),
        ),
        check_vma=False,
    )
```

profile of v0, /device:TPU:0, one launch (start us, length us, event | category | flops | bytes accessed | tf_op | source)
XLA Modules:
  0.0 1537.7 jit_solution(5200302468029986233)
XLA Ops:
  14.9 3.8 fusion.82
  40.6 57.8 %all-gather.7.cloned.1.call-done = bf16[8,1024,768]{2,1,0:T(8,128)(2,1)} async-done(((bf16[8,128,768]{2,1,0:T(8,128)(2,1)}), bf16[8,1024,768]{2,1,0:T(8,128)(2,1)}) %all-gather.7.cloned.1.call-update) | async-done | bytes 12582928 | tf_op jit(solution)/shard_map/all_gather | solution.py:112
  98.4 16.6 %copy.87 = bf16[8,1024,768]{1,2,0:T(8,128)(2,1)} copy(bf16[8,1024,768]{2,1,0:T(8,128)(2,1)} %all-gather.7.cloned.1.call-done) | data formatting | bytes 25165824 | tf_op jit(solution)/shard_map/all_gather | solution.py:112
  115.1 22.4 %broadcast_multiply_fusion = f32[8,12,128,1024]{3,2,1,0:T(8,128)} fusion(bf16[8,1024,12,64]{1,3,2,0:T(8,128)(2,1)} %bitcast.159, bf16[8,128,12,64]{1,0,3,2:T(8,128)(2,1)} %bitcast.166), kind=kOutput, calls=%fused_computation.17 | convolution fusion | flops 1623195648 | bytes 64487424 | tf_op jit(solution)/shard_map/sjhd,sihd->shji/dot_general | solution.py:47
  143.2 5.3 copy.90
  148.5 11.3 fusion.21
  164.7 4.5 broadcast_add_fusion.1
  169.3 5.3 copy.91
  174.6 4.9 reduce_window_sum.44
  179.5 5.6 multiply_bitcast_fusion
  185.1 17.6 %fusion.5 = f32[8,12,1024]{2,1,0:T(8,128)S(1)} fusion(f32[8,12,128,1024]{3,2,1,0:T(8,128)} %broadcast_multiply_fusion, f32[8,128,1024]{2,1,0:T(8,128)} %multiply_bitcast_fusion, pred[8,128,1024]{2,1,0:T(8,128)(4,1)S(1)} %copy-done.10), kind=kLoop, calls=%fused_computation.15 | loop fusion | flops 37650432 | bytes 55967744 | tf_op jit(solution)/shard_map/reduce_max | solution.py:115
  204.6 19.1 %select_reduce_fusion = f32[8,12,1024]{2,1,0:T(8,128)S(1)} fusion(f32[8,12,128,1024]{3,2,1,0:T(8,128)} %broadcast_multiply_fusion, f32[8,12,1024]{2,1,0:T(8,128)} %copy-done.18, f32[8,128,1024]{2,1,0:T(8,128)} %multiply_bitcast_fusion, pred[8,128,1024]{2,1,0:T(8,128)(4,1)} %compare_and_fusion), kind=kLoop, calls=%fused_computation.12 | loop fusion | flops 62816256 | bytes 56360960 | tf_op jit(solution)/shard_map/reduce_sum | solution.py:116
  230.4 6.7 all-gather.11.cloned.1.call-done
  239.1 32.8 %all-gather.13.cloned.1.call-done = f32[64,12,1024]{2,0,1:T(8,128)} async-done(((f32[8,12,1024]{2,0,1:T(8,128)}), f32[64,12,1024]{2,0,1:T(8,128)}) %all-gather.13.cloned.1.call-update) | async-done | bytes 3145744 | tf_op jit(solution)/shard_map/all_gather | solution.py:12
  273.9 27.5 %while.17 = (s32[]{:T(128)}, f32[8,12,1024]{2,1,0:T(8,128)}, f32[8,12,1024]{2,1,0:T(8,128)}, f32[8,8,12,1024]{3,1,0,2:T(8,128)}, f32[8,8,12,1024]{3,1,0,2:T(8,128)}, /*index=5*/s32[]{:T(128)}, s32[]{:T(128)}, s32[]{:T(128)}) while((s32[]{:T(128)}, f32[8,12,1024]{2,1,0:T(8,128)}, f32[8,12,1024]{2,1,0:T(8,128)}, f32[8,8,12,1024]{3,1,0,2:T(8,128)}, ...), condition=%wide.region_7.8_spmd, body=%wide.region_6.7_spmd.sunk | while | flops 589829 | bytes 3932283 | solution.py:18
  301.4 28.9 %fusion.17 = f32[8,12,64,1024]{3,2,1,0:T(8,128)} fusion(bf16[8,128,12,64]{1,0,3,2:T(8,128)(2,1)} %bitcast.184, f32[8,12,128,1024]{3,2,1,0:T(8,128)} %broadcast_multiply_fusion, f32[8,12,1024]{2,1,0:T(8,128)} %get-tuple-element.149, f32[8,12,1024]{2,1,0:T(8,128)} %get-tuple-element.148, f32[8,128,1024]{2,1,0:T(8,128)} %multiply_bitcast_fusion, ...), kind=kOutput, calls=%fused_computation.34 | convolution fusion | flops 1686110208 | bytes 83099648 | tf_op jit(solution)/shard_map/shji,sjhd->sihd/dot_general | solution.py:123
  330.3 24.7 %copy.99 = f32[8,1024,768]{2,1,0:T(8,128)} copy(f32[8,1024,768]{1,2,0:T(8,128)} %bitcast.161) | data formatting | bytes 50331648 | tf_op jit(solution)/shard_map/reshape | solution.py:125
  355.1 157.0 %reduce-scatter.3.cloned.1.call-done = f32[8,128,768]{2,1,0:T(8,128)} async-done(((f32[8,1024,768]{2,1,0:T(8,128)}), f32[8,128,768]{2,1,0:T(8,128)}) %reduce-scatter.3.cloned.1.call-update) | async-done | bytes 3145744 | tf_op jit(solution)/shard_map/reduce_scatter | solution.py:126
  517.0 11.4 fusion.73
  528.4 15.6 %convert_reduce_fusion = (f32[3072]{0:T(1024)}, bf16[1024,3072]{1,0:T(8,128)(2,1)S(1)}) fusion(f32[1024,3072]{1,0:T(8,128)} %fusion.73, f32[3072]{0:T(1024)S(1)} %copy-done.51, bf16[1024,768]{1,0:T(8,128)(2,1)S(1)} %bitcast.168, bf16[3072,768]{1,0:T(8,128)(2,1)} %param.32), kind=kOutput, calls=%fused_computation.29 | convolution fusion | flops 4904186880 | bytes 25190400 | tf_op jit(solution)/shard_map/dot_general | solution.py:138
  544.0 6.2 multiply_reduce_fusion.1
  556.6 72.2 %all-gather.9.cloned.1.call-done = bf16[8,1024,768]{2,1,0:T(8,128)(2,1)} async-done(((bf16[8,128,768]{2,1,0:T(8,128)(2,1)}), bf16[8,1024,768]{2,1,0:T(8,128)(2,1)}) %all-gather.9.cloned.1.call-update) | async-done | bytes 12582928 | tf_op jit(solution)/shard_map/all_gather | solution.py:159
  628.8 17.1 %copy.100 = bf16[8,1024,768]{1,2,0:T(8,128)(2,1)} copy(bf16[8,1024,768]{2,1,0:T(8,128)(2,1)} %all-gather.9.cloned.1.call-done) | data formatting | bytes 25165824 | tf_op jit(solution)/shard_map/all_gather | solution.py:159
  646.0 45.0 %multiply_reduce_fusion = (f32[8,12,1024]{2,1,0:T(8,128)}, f32[8,12,128,1024]{3,2,1,0:T(8,128)}) fusion(f32[8,12,1024]{2,1,0:T(8,128)} %get-tuple-element.149, f32[8,12,1024]{2,1,0:T(8,128)} %get-tuple-element.148, f32[8,12,128,1024]{3,2,1,0:T(8,128)} %broadcast_multiply_fusion, f32[8,128,1024]{2,1,0:T(8,128)} %multiply_bitcast_fusion, ...), kind=kOutput, calls=%fused_computation.10 | convolution fusion | flops 1698594816 | bytes 121241600 | tf_op jit(solution)/shard_map/sihd,sjhd->shji/dot_general | solution.py:166
  691.1 54.7 %all-reduce.6.cloned.1.call-done = f32[8,12,1024]{2,1,0:T(8,128)} async-done(((f32[8,12,1024]{2,1,0:T(8,128)}), f32[8,12,1024]{2,1,0:T(8,128)}) %all-reduce.6.cloned.1.call-update) | async-done | bytes 393232 | tf_op jit(solution)/shard_map/psum | solution.py:170
  745.7 53.9 %fusion.78 = (f32[8,128,1024]{2,1,0:T(8,128)S(1)}, f32[8,12,128,1024]{3,2,1,0:T(8,128)}) fusion(f32[8,12,128,1024]{3,2,1,0:T(8,128)} %get-tuple-element.212, f32[8,12,1024]{2,1,0:T(8,128)} %all-reduce.6.cloned.1.call-done, f32[8,12,1024]{2,1,0:T(8,128)} %get-tuple-element.149, f32[8,12,1024]{2,1,0:T(8,128)} %get-tuple-element.148, ...), kind=kLoop, calls=%fused_computation.142 | loop fusion | flops 99614720 | bytes 161611776 | tf_op jit(solution)/shard_map/reduce_sum | solution.py:172
  804.6 5.3 copy.102
  817.3 4.5 broadcast_add_fusion
  821.8 5.3 copy.103
  827.2 4.9 reduce_window_sum.46
  832.0 24.9 %slice.95 = bf16[8,11,128,1024]{3,2,1,0:T(8,128)(2,1)} slice(f32[8,12,128,1024]{3,2,1,0:T(8,128)} %get-tuple-element.197), slice={[0:8], [1:12], [0:128], [0:1024]} | slice | bytes 46137344 | tf_op jit(solution)/shard_map/slice | solution.py:176
  857.0 7.0 fusion.19
  864.0 20.5 %broadcast_multiply_fusion.1 = f32[8,12,64,1024]{3,2,1,0:T(8,128)} fusion(bf16[8,11,128,1024]{3,2,1,0:T(8,128)(2,1)} %slice.95, bf16[8,1,128,1024]{3,2,1,0:T(8,128)(2,1)S(1)} %fusion.19, bf16[8,128,12,64]{1,0,3,2:T(8,128)(2,1)S(1)} %bitcast.167), kind=kOutput, calls=%fused_computation.30 | convolution fusion | flops 1629487104 | bytes 51904512 | tf_op jit(solution)/shard_map/shji,sjhd->sihd/dot_general | solution.py:179
  884.5 24.7 %copy.105 = f32[8,1024,768]{2,1,0:T(8,128)} copy(f32[8,1024,768]{1,2,0:T(8,128)} %bitcast.158) | data formatting | bytes 50331648 | tf_op jit(solution)/shard_map/reshape | solution.py:186
  909.4 4.9 fusion.83
  914.3 12.9 fusion.72
  927.3 10.8 fusion.74
  938.1 29.8 %convert_reduce_fusion.4 = (f32[12,64]{1,0:T(8,128)}, bf16[8,128,12,64]{1,3,2,0:T(8,128)(2,1)}) fusion(bf16[8,1024,12,64]{1,3,2,0:T(8,128)(2,1)} %bitcast.171, f32[8,12,1024]{2,1,0:T(8,128)} %get-tuple-element.149, f32[8,12,1024]{2,1,0:T(8,128)} %get-tuple-element.148, f32[8,12,128,1024]{3,2,1,0:T(8,128)} %broadcast_multiply_fusion, ...), kind=kOutput, calls=%fused_computation.76 | convolution fusion | flops 1688468736 | bytes 70519808 | tf_op jit(solution)/shard_map/shji,sihd->sjhd/dot_general | solution.py:206
  974.9 16.1 %fusion.54 = bf16[8,128,12,64]{1,3,2,0:T(8,128)(2,1)S(1)} fusion(bf16[8,1024,12,64]{1,3,2,0:T(8,128)(2,1)} %bitcast.160, bf16[8,11,128,1024]{3,2,1,0:T(8,128)(2,1)} %slice.95, bf16[8,1,128,1024]{3,2,1,0:T(8,128)(2,1)} %copy-done.15), kind=kOutput, calls=%fused_computation.101 | convolution fusion | flops 1624768512 | bytes 39321600 | tf_op jit(solution)/shard_map/shji,sihd->sjhd/dot_general | solution.py:194
  996.4 69.1 %reduce-scatter.5.cloned.1.call-done = f32[8,128,768]{2,1,0:T(8,128)} async-done(((f32[8,1024,768]{2,1,0:T(8,128)}), f32[8,128,768]{2,1,0:T(8,128)}) %reduce-scatter.5.cloned.1.call-update) | async-done | bytes 3145744 | tf_op jit(solution)/shard_map/reduce_scatter | solution.py:188
  1069.8 6.3 fusion.46
  1078.4 14.9 add_convert_fusion
  1094.7 7.7 fusion.75
  1104.6 42.3 %all-reduce.1 = (f32[768]{0:T(1024)}, f32[768]{0:T(1024)}, f32[768]{0:T(1024)}, f32[768]{0:T(1024)}, f32[768]{0:T(1024)}, /*index=5*/f32[768]{0:T(1024)}, f32[768]{0:T(1024)}, f32[3072]{0:T(1024)}, f32[768]{0:T(1024)}) all-reduce(f32[768]{0:T(1024)} %get-tuple-element.194, ...), channel_id=1, replica_groups=mesh['rows'=4,'cols'=8] {'rows','cols'}, use_global_device_ids=true, to_apply=%region_23.24 | all-reduce | flops 9216 | bytes 73728 | tf_op jit(solution)/shard_map/psum | solution.py:218
  1147.6 5.8 add_add_fusion.2
  1153.4 356.1 %all-reduce.8.cloned.1.call-done = (f32[768,2304]{1,0:T(8,128)}, f32[768,768]{1,0:T(8,128)}, f32[768,3072]{1,0:T(8,128)}, f32[3072,768]{1,0:T(8,128)}) async-done(((f32[768,2304]{1,0:T(8,128)}, f32[768,768]{1,0:T(8,128)}, f32[768,3072]{1,0:T(8,128)}, f32[3072,768]{1,0:T(8,128)}), (f32[768,2304]{1,0:T(8,128)}, f32[768,768]{1,0:T(8,128)}, f32[768,3072]{1,0:T(8,128)}, ...) | async-done | bytes 28311568 | tf_op jit(solution)/shard_map/psum | solution.py:218
  1509.5 6.6 copy.163
  1517.5 9.3 copy.165
  (220 shorter events, 131.9 us)
Async XLA Ops:
  7.2 7.7 copy-start
  7.2 91.2 %all-gather.7.cloned.1.call-start = ((), (), s32[]{:S(2)}) async-start(), calls=%async_computation.2 | async-start | bytes 14155776 | tf_op jit(solution)/shard_map/all_gather | solution.py:112
  7.2 5.1 copy-start.1
  18.7 4.7 copy-start.17
  23.5 213.6 %all-gather.11.cloned.1.call-start = ((), (), s32[]{:S(2)}) async-start(), calls=%async_computation.7 | async-start | bytes 3538944 | tf_op jit(solution)/shard_map/all_gather | solution.py:12
  35.7 143.8 %copy-start.45 = (pred[8,128]{1,0:T(8,128)(4,1)}, pred[8,128]{1,0:T(8,128)(4,1)S(1)}, u32[]{:S(2)}) copy-start(pred[8,128]{1,0:T(8,128)(4,1)S(1)} %fusion.63) | copy-start | bytes 3076
  36.4 143.1 %copy-start.31 = (s32[8,128]{1,0:T(8,128)}, s32[8,128]{1,0:T(8,128)S(1)}, u32[]{:S(2)}) copy-start(s32[8,128]{1,0:T(8,128)S(1)} %constant_dynamic-slice_fusion.2) | copy-start | bytes 12292
  179.5 5.7 copy-start.10
  204.6 67.3 %all-gather.13.cloned.1.call-start = ((), (), s32[]{:S(2)}) async-start(), calls=%async_computation.8 | async-start | bytes 3538944 | tf_op jit(solution)/shard_map/all_gather | solution.py:12
  224.7 287.3 %reduce-scatter.3.cloned.1.call-start = ((), (), s32[]{:S(2)}) async-start(), calls=%async_computation.3 | async-start | bytes 28311552 | tf_op jit(solution)/shard_map/reduce_scatter | solution.py:126
  355.0 159.3 %copy-start.53 = (f32[768]{0:T(1024)S(1)}, f32[768]{0:T(1024)}, u32[]{:S(2)}) copy-start(f32[768]{0:T(1024)} %param.25) | copy-start | bytes 9220
  355.0 273.8 %all-gather.9.cloned.1.call-start = ((), (), s32[]{:S(2)}) async-start(), calls=%async_computation.4 | async-start | bytes 14155776 | tf_op jit(solution)/shard_map/all_gather | solution.py:159
  516.3 33.9 %copy-start.5 = (f32[1024,768]{1,0:T(8,128)}, f32[1024,768]{1,0:T(8,128)S(1)}, u32[]{:S(2)}) copy-start(f32[1024,768]{1,0:T(8,128)S(1)} %get-tuple-element.209) | copy-start | bytes 9437188
  516.4 33.9 %copy-start.27 = (f32[1024]{0:T(1024)}, f32[1024]{0:T(1024)S(1)}, u32[]{:S(2)}) copy-start(f32[1024]{0:T(1024)S(1)} %broadcast_multiply_fusion.3) | copy-start | bytes 12292
  516.9 33.4 %copy-start.29 = (f32[1024]{0:T(1024)}, f32[1024]{0:T(1024)S(1)}, u32[]{:S(2)}) copy-start(f32[1024]{0:T(1024)S(1)} %fusion.64) | copy-start | bytes 12292
  516.9 11.5 copy-start.12
  516.9 11.4 copy-start.51
  517.0 27.1 %slice-start.3 = ((s8[4718592]{0:T(1024)(128)(4,1)}), s8[4194304]{0:T(1024)(128)(4,1)S(1)}, s32[]{:S(2)}) async-start(s8[4718592]{0:T(1024)(128)(4,1)} %bitcast.192), calls=%async_computation.13 | async-start | bytes 8388608
  528.4 15.7 %slice-start.4 = ((s8[4718592]{0:T(1024)(128)(4,1)}), s8[524288]{0:T(1024)(128)(4,1)S(1)}, s32[]{:S(2)}) async-start(s8[4718592]{0:T(1024)(128)(4,1)} %bitcast.192), calls=%async_computation.14 | async-start | bytes 1048576
  544.0 6.2 copy-start.16
  551.8 4.7 copy-start.7
  551.8 4.7 copy-start.42
  556.6 189.2 %all-reduce.6.cloned.1.call-start = ((), (), s32[]{:S(2)}) async-start(), calls=%async_computation.5 | async-start | bytes 1048576 | tf_op jit(solution)/shard_map/psum | solution.py:170
  691.0 374.6 %reduce-scatter.5.cloned.1.call-start = ((), (), s32[]{:S(2)}) async-start(), calls=%async_computation.6 | async-start | bytes 28311552 | tf_op jit(solution)/shard_map/reduce_scatter | solution.py:188
  832.0 24.9 %copy-start.32 = (s32[8,128]{1,0:T(8,128)S(1)}, s32[8,128]{1,0:T(8,128)}, u32[]{:S(2)}) copy-start(s32[8,128]{1,0:T(8,128)} %copy-done.31) | copy-start | bytes 12292
  832.0 24.9 %copy-start.46 = (pred[8,128]{1,0:T(8,128)(4,1)S(1)}, pred[8,128]{1,0:T(8,128)(4,1)}, u32[]{:S(2)}) copy-start(pred[8,128]{1,0:T(8,128)(4,1)} %copy-done.45) | copy-start | bytes 3076
  857.0 7.0 copy-start.11
  864.0 20.5 %copy-start.15 = (bf16[8,1,128,1024]{3,2,1,0:T(8,128)(2,1)}, bf16[8,1,128,1024]{3,2,1,0:T(8,128)(2,1)S(1)}, u32[]{:S(2)}) copy-start(bf16[8,1,128,1024]{3,2,1,0:T(8,128)(2,1)S(1)} %fusion.19) | copy-start | bytes 6291460
  909.2 5.0 copy-start.28
  909.3 5.0 copy-start.30
  909.3 5.0 copy-start.34
  909.3 5.0 copy-start.40
  909.3 600.2 %all-reduce.8.cloned.1.call-start = ((), (), s32[]{:S(2)}) async-start(), calls=%async_computation.9 | async-start | bytes 56623104 | tf_op jit(solution)/shard_map/psum | solution.py:218
  909.3 4.9 copy-start.6
  909.4 17.9 %slice-start.5 = ((s8[12582912]{0:T(1024)(128)(4,1)}), s8[4194304]{0:T(1024)(128)(4,1)S(1)}, s32[]{:S(2)}) async-start(s8[12582912]{0:T(1024)(128)(4,1)} %bitcast.195), calls=%async_computation.15 | async-start | bytes 8388608
  914.3 12.9 copy-start.13
  914.3 12.9 copy-start.52
  914.3 12.9 slice-start.6
  914.3 12.9 slice-start.7
  1078.4 16.3 %copy-start.36 = (f32[1024]{0:T(1024)S(1)}, f32[1024]{0:T(1024)}, u32[]{:S(2)}) copy-start(f32[1024]{0:T(1024)} %copy-done.35) | copy-start | bytes 12292
  1078.4 16.3 %copy-start.41 = (f32[768]{0:T(1024)S(1)}, f32[768]{0:T(1024)}, u32[]{:S(2)}) copy-start(f32[768]{0:T(1024)} %param.26) | copy-start | bytes 9220
  1094.7 7.7 copy-start.44
  1094.7 7.7 copy-start.3
  1094.7 7.7 copy-start.38
  1509.5 6.6 copy-start.19
  1516.1 10.7 slice-start
  1517.5 9.3 slice-start.1
  1517.5 9.3 slice-start.2
  (23 other events, 54.8 us)
Sparse Core Ops, SparseCore 0:
  23.6 74.8 all-gather.6
  204.7 32.3 all-gather.10
  239.5 32.3 all-gather.12
  355.1 156.8 reduce-scatter.2
  556.7 72.1 all-gather.8
  691.1 54.5 all-reduce.5
  909.4 156.1 reduce-scatter.4
  1076.2 433.2 all-reduce.7
where the time goes:
time: 1550 us; the launch traced here: 1540 us
  waiting for transfers between devices  807 us (52%)
  matrix products  262 us (17%)
  local copies, waits for them, and re-layouts  228 us (15%)
  other arithmetic  184 us (12%)
  blocking collectives  42.3 us (3%)
    psum x1, waiting for transfers between devices, per_device(): lax.psum((g_w_qkv, g_q_bias, g_v_bias, g_attn_gain, g_attn_shift), ('rows...  356 us
    reduce_scatter x1, waiting for transfers between devices, per_device(): lax.psum_scatter(partial_out, 'cols', scatter_dimension=1, tiled=True)  157 us
    all_gather x1, waiting for transfers between devices, per_device(): grad_out_all = lax.all_gather(grad_attended, 'cols', axis=1, tiled=True)  72.2 us
    reduce_scatter x1, waiting for transfers between devices, per_device(): lax.psum_scatter(grad_q_part, 'cols', scatter_dimension=1, tiled=True)  69.1 us
    all_gather x1, waiting for transfers between devices, per_device(): queries_all = lax.all_gather(queries, 'cols', axis=1, tiled=True)  57.8 us
    psum x1, waiting for transfers between devices, per_device(): delta = lax.psum(local_delta, 'cols')  54.7 us
    reduce_sum x1, other arithmetic, per_device(): grad_carried = -(8.0 / LEN) * jnp.sum(grad_logits, axis=1)  53.9 us
    unnamed x136, local copies, waits for them, and re-layouts  49.8 us
  transfers between devices with their start and end apart: 8, of which 8 were waited for; matrix products, arithmetic and copies ran while one was open for 11% of the time, Pallas kernels for 0%

commit v1 on v0

v1 whole, which is shorter than its diff:
```python
import jax
import jax.numpy as jnp
from jax import lax
from jax.sharding import PartitionSpec as P

HEADS = 12
HDIM = 64
BF = jnp.bfloat16
F32 = jnp.float32


def to_whole(value, copies):
    if copies > 1:
        value = jnp.repeat(value, copies, axis=0)
    return lax.all_to_all(value, "cols", 0, 1, tiled=True)


def to_parts(value, copies):
    parts = lax.all_to_all(value, "cols", 1, 0, tiled=True)
    return parts[::copies] if copies > 1 else parts


def dot(a, b, dims=((1,), (0,))):
    return lax.dot_general(a, b, (dims, ((), ())), preferred_element_type=F32)


def norm_parts(values):
    average = jnp.mean(values, axis=-1, keepdims=True)
    centered = values - average
    scale = lax.rsqrt(jnp.mean(centered * centered, axis=-1, keepdims=True) + 1e-05)
    return centered * scale, scale


def norm_back(grad, normal, scale, gain):
    weighted = grad * gain
    inner = jnp.mean(weighted * normal, axis=-1, keepdims=True)
    return scale * (weighted - jnp.mean(weighted, axis=-1, keepdims=True) - normal * inner)


def gelu_tanh(values):
    return jax.nn.gelu(values, approximate=True)


def heads_of(values):
    return values.reshape(values.shape[0], HEADS, HDIM)


def score_parts(queries, keys, segs):
    length = queries.shape[0]
    scores = jnp.einsum(
        "ihd,jhd->hij", heads_of(queries), heads_of(keys), preferred_element_type=F32
    ) * HDIM ** (-0.5)
    pos = jnp.arange(length, dtype=jnp.int32)
    starts = jnp.concatenate([segs[:-1] != segs[1:], jnp.ones((1,), dtype=bool)])
    same = segs[:, None] == segs[None, :]
    allowed = same & (pos[:, None] <= pos[None, :])
    picked = same & (pos[:, None] < pos[None, :]) & ~starts[None, :]
    selected = jnp.where(picked, jax.nn.relu(scores[0]), 0.0)
    carried = lax.cumsum(selected, axis=0, reverse=True) - selected
    logits = jnp.where(allowed[None], scores - 8.0 / length * carried[None], -1e30)
    return scores, logits, allowed, picked


def attend(queries, keys, values, segs):
    scores, logits, allowed, picked = score_parts(queries, keys, segs)
    peak = jnp.max(logits, axis=2, keepdims=True)
    expon = jnp.where(allowed[None], jnp.exp(logits - peak), 0.0)
    total = jnp.sum(expon, axis=2, keepdims=True)
    probs = (expon / total).astype(BF)
    mixed = jnp.einsum("hij,jhd->ihd", probs, heads_of(values), preferred_element_type=F32)
    return mixed.reshape(queries.shape), peak + jnp.log(total)


def attend_back(queries, keys, values, segs, stats, grad):
    length = queries.shape[0]
    scores, logits, allowed, picked = score_parts(queries, keys, segs)
    probs = jnp.where(allowed[None], jnp.exp(logits - stats), 0.0)
    grad_probs = jnp.einsum(
        "ihd,jhd->hij", heads_of(grad), heads_of(values), preferred_element_type=F32
    )
    delta = jnp.sum(probs * grad_probs, axis=2, keepdims=True)
    grad_logits = probs * (grad_probs - delta)
    grad_carried = -(8.0 / length) * jnp.sum(grad_logits, axis=0)
    grad_selected = lax.cumsum(grad_carried, axis=0) - grad_carried
    extra = jnp.where(picked & (scores[0] > 0), grad_selected, 0.0)
    grad_scores = jnp.concatenate([grad_logits[:1] + extra[None], grad_logits[1:]], 0).astype(BF)
    scale = HDIM ** (-0.5)
    dq = jnp.einsum("hij,jhd->ihd", grad_scores, heads_of(keys), preferred_element_type=F32)
    dk = jnp.einsum("hij,ihd->jhd", grad_scores, heads_of(queries), preferred_element_type=F32)
    dv = jnp.einsum("hij,ihd->jhd", probs.astype(BF), heads_of(grad), preferred_element_type=F32)
    shape = queries.shape
    return tuple(g.astype(BF).reshape(shape) for g in (dq * scale, dk * scale, dv))


def layer(tokens, segs, cotangent, weights):
    (w_qkv, q_bias, v_bias, w_out, out_bias, attn_gain, attn_shift, mlp_gain, mlp_shift,
     w_up, up_bias, w_down, down_bias) = weights
    width = tokens.shape[1]
    inputs = tokens.astype(F32)
    normal_one, scale_one = norm_parts(inputs)
    normed = (normal_one * attn_gain + attn_shift).astype(BF)
    projected = dot(normed, w_qkv)
    queries = (projected[:, :width] + q_bias).astype(BF)
    keys = projected[:, width : 2 * width].astype(BF)
    values = (projected[:, 2 * width :] + v_bias).astype(BF)
    mixed, stats = attend(queries, keys, values, segs)
    attended = mixed.astype(BF)
    residual = inputs + dot(attended, w_out) + out_bias
    normal_two, scale_two = norm_parts(residual)
    normed_two = (normal_two * mlp_gain + mlp_shift).astype(BF)
    upper = dot(normed_two, w_up) + up_bias
    act, gelu_back = jax.vjp(gelu_tanh, upper)
    act = act.astype(BF)
    output = (residual + dot(act, w_down) + down_bias).astype(BF)
    grad_top = cotangent.astype(F32)
    g_down_bias = jnp.sum(grad_top, axis=0)
    g_w_down = dot(act, cotangent, ((0,), (0,)))
    grad_upper = gelu_back(dot(cotangent, w_down, ((1,), (1,))))[0].astype(BF)
    g_up_bias = jnp.sum(grad_upper.astype(F32), axis=0)
    g_w_up = dot(normed_two, grad_upper, ((0,), (0,)))
    grad_two = dot(grad_upper, w_up, ((1,), (1,)))
    g_mlp_gain = jnp.sum(grad_two * normal_two, axis=0)
    g_mlp_shift = jnp.sum(grad_two, axis=0)
    grad_residual = grad_top + norm_back(grad_two, normal_two, scale_two, mlp_gain)
    grad_branch = grad_residual.astype(BF)
    g_out_bias = jnp.sum(grad_branch.astype(F32), axis=0)
    g_w_out = dot(attended, grad_branch, ((0,), (0,)))
    grad_attended = dot(grad_branch, w_out, ((1,), (1,))).astype(BF)
    dq, dk, dv = attend_back(queries, keys, values, segs, stats, grad_attended)
    g_q_bias = jnp.sum(dq.astype(F32), axis=0)
    g_v_bias = jnp.sum(dv.astype(F32), axis=0)
    grad_proj = jnp.concatenate([dq, dk, dv], axis=1)
    g_w_qkv = dot(normed, grad_proj, ((0,), (0,)))
    grad_one = dot(grad_proj, w_qkv, ((1,), (1,)))
    g_attn_gain = jnp.sum(grad_one * normal_one, axis=0)
    g_attn_shift = jnp.sum(grad_one, axis=0)
    grad_tokens = grad_residual + norm_back(grad_one, normal_one, scale_one, attn_gain)
    return output, grad_tokens, (
        g_w_qkv, g_q_bias, g_v_bias, g_w_out, g_out_bias, g_attn_gain, g_attn_shift,
        g_mlp_gain, g_mlp_shift, g_w_up, g_up_bias, g_w_down, g_down_bias)


def summed_grads(grads, copies):
    grads = [g / copies for g in grads] if copies > 1 else list(grads)
    matrices = [i for i, g in enumerate(grads) if g.ndim == 2]
    vectors = [i for i, g in enumerate(grads) if g.ndim == 1]
    big = lax.psum([grads[i].astype(BF) for i in matrices], ("rows", "cols"))
    small = lax.psum(jnp.concatenate([grads[i] for i in vectors]), ("rows", "cols"))
    out = [None] * len(grads)
    for i, g in zip(matrices, big):
        out[i] = g.astype(F32)
    at = 0
    for i in vectors:
        out[i] = small[at : at + grads[i].shape[0]]
        at += grads[i].shape[0]
    return out


def per_device(tokens, segment_ids, cotangent, *weights):
    seqs = tokens.shape[0]
    cols = lax.axis_size("cols")
    copies = max(1, cols // seqs)
    held = max(1, seqs // cols)
    tokens_whole = to_whole(tokens, copies)
    cotangent_whole = to_whole(cotangent, copies)
    first = (lax.axis_index("cols") // copies) * held
    segs = lax.dynamic_slice_in_dim(segment_ids, first, held, 0)
    results = [
        layer(tokens_whole[s], segs[s], cotangent_whole[s], weights) for s in range(held)
    ]
    output = jnp.stack([r[0] for r in results])
    grad_tokens = jnp.stack([r[1] for r in results])
    grads = [sum(parts[1:], parts[0]) for parts in zip(*[r[2] for r in results])]
    return (
        to_parts(output, copies),
        to_parts(grad_tokens.astype(BF), copies).astype(F32),
        *summed_grads(grads, copies),
    )


def solution(mesh):
    placed = (P("rows", "cols", None), P("rows", None), P("rows", "cols", None)) + (P(),) * 13
    return jax.shard_map(
        per_device,
        mesh=mesh,
        in_specs=placed,
        out_specs=(P("rows", "cols", None), P("rows", "cols", None)) + (P(),) * 13,
        check_vma=False,
    )
```

time: 1550 us -> 772 us (0.50)
  waiting for transfers between devices: 807 us -> 120 us
  local copies, waits for them, and re-layouts: 228 us -> 129 us
  matrix products: 262 us -> 227 us
  other arithmetic: 184 us -> 208 us
  starting transfers between devices: 0.33 us -> 18.7 us
    psum x2 -> x1, waiting for transfers between devices: 411 us -> 85.2 us  [summed_grads(): big = lax.psum([grads[i].astype(BF) for i in matrices], ('rows', 'cols'))]
    reduce_scatter x2 -> x0, waiting for transfers between devices: 226 us -> none  [the longest x1 157 us: per_device(): lax.psum_scatter(partial_out, 'cols', scatter_dimension=1, tiled=True)]
    all_gather x4 -> x0, waiting for transfers between devices: 169 us -> none  [the longest x1 72.2 us: per_device(): grad_out_all = lax.all_gather(grad_attended, 'cols', axis=1, tiled=True)]
    reshape x4 -> x0, local copies, waits for them, and re-layouts: 54.6 us -> none  [the longest x1 24.7 us: per_device(): grad_q_part = (jnp.einsum('shji,sjhd->sihd', grad_scores, split_heads(key...]
    dot_general x18, matrix products: 262 us -> 227 us  [the longest x12 96.5 us: dot(): return lax.dot_general(a, b, (dims, ((), ())), preferred_element_type=F32)]
    all_to_all x0 -> x4, waiting for transfers between devices: none -> 34.5 us  [the longest x2 34.4 us: to_whole(): return lax.all_to_all(value, 'cols', 0, 1, tiled=True)]
    all_gather x2 -> x0, local copies, waits for them, and re-layouts: 33.8 us -> none  [the longest x1 17.1 us: per_device(): grad_out_all = lax.all_gather(grad_attended, 'cols', axis=1, tiled=True)]
    unnamed x3 -> x5, other arithmetic: 0.01 us -> 24.9 us
  transfers between devices with their start and end apart: 8 -> 5, of which waited for: 8 -> 3; matrix products, arithmetic and copies ran while one was open for 11% -> 17% of each run, Pallas kernels for 0% -> 0%
where the time goes in v1:
time: 772 us; the launch traced here: 761 us
  matrix products  227 us (29%)
  other arithmetic  208 us (27%)
  local copies, waits for them, and re-layouts  129 us (17%)
  waiting for transfers between devices  120 us (16%)
  blocking collectives  43 us (6%)
  starting transfers between devices  18.7 us (2%)
  between operations  15.1 us (2%)
    dot_general x12, matrix products, dot(): return lax.dot_general(a, b, (dims, ((), ())), preferred_element_type=F32)  96.5 us
    psum x1, waiting for transfers between devices, summed_grads(): big = lax.psum([grads[i].astype(BF) for i in matrices], ('rows', 'cols'))  85.2 us
    reduce_sum x1, other arithmetic, attend_back(): grad_carried = -(8.0 / length) * jnp.sum(grad_logits, axis=0)  54.2 us
    unnamed x111, local copies, waits for them, and re-layouts  48.7 us
    psum x1, blocking collectives, summed_grads(): lax.psum(jnp.concatenate([grads[i] for i in vectors]), ('rows', 'cols'))  43 us
    dot_general x1, matrix products, attend_back(): jnp.einsum('ihd,jhd->hij', heads_of(grad), heads_of(values), preferred_el...  38.8 us
    all_to_all x2, waiting for transfers between devices, to_whole(): return lax.all_to_all(value, 'cols', 0, 1, tiled=True)  34.4 us
    reduce_sum x1, other arithmetic, attend(): total = jnp.sum(expon, axis=2, keepdims=True)  25.9 us
  transfers between devices with their start and end apart: 5, of which 3 were waited for; matrix products, arithmetic and copies ran while one was open for 17% of the time, Pallas kernels for 0%

profile of v1, /device:TPU:0, one launch (start us, length us, event | category | flops | bytes accessed | tf_op | source)
XLA Modules:
  0.0 760.6 jit_solution(3493387562594989184)
XLA Ops:
  7.2 5.4 all-to-all-start
  13.6 20.2 %all-to-all-done = bf16[8,128,768]{2,1,0:T(8,128)(2,1)} async-done(((bf16[8,128,768]{2,1,0:T(8,128)(2,1)}), bf16[8,128,768]{2,1,0:T(8,128)(2,1)}, u32[]{:S(2)}, u32[]{:S(2)}) %all-to-all-start) | async-done | bytes 1572896 | tf_op jit(solution)/shard_map/all_to_all | solution.py:15
  33.8 4.3 all-to-all-start.2
  44.9 14.2 %all-to-all-done.2 = bf16[8,128,768]{2,1,0:T(8,128)(2,1)} async-done(((bf16[8,128,768]{2,1,0:T(8,128)(2,1)}), bf16[8,128,768]{2,1,0:T(8,128)(2,1)}, u32[]{:S(2)}, u32[]{:S(2)}) %all-to-all-start.2) | async-done | bytes 1572896 | tf_op jit(solution)/shard_map/all_to_all | solution.py:15
  64.8 6.2 fusion.41
  82.3 21.0 %broadcast_multiply_fusion = f32[12,1024,1024]{2,1,0:T(8,128)} fusion(bf16[1024,12,64]{0,2,1:T(8,128)(2,1)} %bitcast.102, bf16[1024,12,64]{0,2,1:T(8,128)(2,1)} %bitcast.100), kind=kOutput, calls=%fused_computation.12 | convolution fusion | flops 1623195648 | bytes 53477376 | tf_op jit(solution)/shard_map/ihd,jhd->hij/dot_general | solution.py:50
  106.5 10.2 %fusion.18 = f32[1024,8,128]{0,1,2:T(8,128)S(1)} fusion(f32[1024,8,128]{0,2,1:T(8,128)S(1)} %bitcast.94), kind=kOutput, calls=%fused_computation.41 | output fusion | flops 133169152 | bytes 8388608 | tf_op jit(solution)/shard_map/reduce-window
  126.7 4.9 broadcast_multiply_fusion.2
  131.6 21.2 %fusion.1 = f32[12,1024]{1,0:T(8,128)S(1)} fusion(f32[12,1024,1024]{2,1,0:T(8,128)} %broadcast_multiply_fusion, f32[1024,1024]{1,0:T(8,128)} %broadcast_multiply_fusion.2, pred[1024,1024]{1,0:T(8,128)(4,1)S(1)} %copy-done.2), kind=kLoop, calls=%fused_computation.8 | loop fusion | flops 37736448 | bytes 55623680 | tf_op jit(solution)/shard_map/reduce_max | solution.py:66
  152.9 25.9 %fusion = f32[12,1024]{1,0:T(8,128)S(1)} fusion(f32[12,1024,1024]{2,1,0:T(8,128)} %broadcast_multiply_fusion, f32[12,1024]{1,0:T(8,128)S(1)} %fusion.1, f32[1024,1024]{1,0:T(8,128)} %broadcast_multiply_fusion.2, pred[1024,1024]{1,0:T(8,128)(4,1)S(1)} %copy-done.2), kind=kLoop, calls=%fused_computation.7 | loop fusion | flops 62902272 | bytes 55672832 | tf_op jit(solution)/shard_map/reduce_sum | solution.py:68
  179.4 20.8 %fusion.27 = bf16[12,64,1024]{2,1,0:T(8,128)(2,1)} fusion(bf16[1024,12,64]{0,2,1:T(8,128)(2,1)} %bitcast.104, f32[12,1024,1024]{2,1,0:T(8,128)} %broadcast_multiply_fusion, f32[12,1024]{1,0:T(8,128)S(1)} %fusion, f32[12,1024]{1,0:T(8,128)S(1)} %fusion.1, f32[1024,1024]{1,0:T(8,128)} %broadcast_multiply_fusion.2, pred[1024,1024]{1,0:T(8,128)(4,1)S(1)} %copy-done.2), kind=kOutput, calls=%fused_computation.81 | convolution fusion | flops 1686896640 | bytes 58818560 | tf_op jit(solution)/shard_map/hij,jhd->ihd/dot_general | solution.py:70
  200.2 4.5 fusion.45
  205.2 5.6 fusion.42
  210.8 12.1 %convolution_convert_fusion = bf16[3072,768]{1,0:T(8,128)(2,1)} fusion(bf16[1024,768]{1,0:T(8,128)(2,1)} %bitcast.16, f32[1024,3072]{1,0:T(8,128)S(1)} %fusion.42, f32[3072]{0:T(1024)S(1)} %copy-done.38), kind=kOutput, calls=%fused_computation.29 | convolution fusion | flops 4865654784 | bytes 18886656 | tf_op jit(solution)/shard_map/dot_general | solution.py:24
  222.9 17.1 %convert_reduce_fusion = (f32[3072]{0:T(1024)}, bf16[1024,3072]{1,0:T(8,128)(2,1)}) fusion(f32[1024,3072]{1,0:T(8,128)S(1)} %fusion.42, f32[3072]{0:T(1024)S(1)} %copy-done.38, bf16[1024,768]{1,0:T(8,128)(2,1)} %bitcast.16, bf16[3072,768]{1,0:T(8,128)(2,1)} %param.30), kind=kOutput, calls=%fused_computation.25 | convolution fusion | flops 4904186880 | bytes 25190400 | tf_op jit(solution)/shard_map/dot_general | solution.py:24
  240.0 10.5 %fusion.47 = (f32[768]{0:T(1024)}, f32[1024,768]{1,0:T(8,128)}) fusion(bf16[1024,3072]{1,0:T(8,128)(2,1)} %get-tuple-element.84, bf16[768,3072]{1,0:T(8,128)(2,1)} %param.28), kind=kOutput, calls=%fused_computation.126 | convolution fusion | flops 4832623616 | bytes 14158848 | tf_op jit(solution)/shard_map/dot_general | solution.py:24
  250.5 7.0 convolution_convert_fusion.1
  257.5 3.6 copy.97
  261.2 4.6 multiply_reduce_fusion.1
  274.6 24.1 %convert_reduce_fusion.3 = (f32[12,64]{1,0:T(8,128)}, bf16[12,64,1024]{2,1,0:T(8,128)(2,1)}) fusion(bf16[1024,12,64]{0,2,1:T(8,128)(2,1)S(1)} %bitcast.111, f32[12,1024]{1,0:T(8,128)S(1)} %copy-done.19, f32[12,1024,1024]{2,1,0:T(8,128)} %broadcast_multiply_fusion, f32[1024,1024]{1,0:T(8,128)S(1)} %copy-done.1, pred[1024,1024]{1,0:T(8,128)(4,1)S(1)} %copy-done.3), kind=kOutput, calls=%fused_computation.56 | convolution fusion | flops 1675885824 | bytes 58772480 | tf_op jit(solution)/shard_map/hij,ihd->jhd/dot_general | solution.py:90
  298.7 38.8 %multiply_reduce_fusion = (f32[12,1024]{1,0:T(8,128)}, f32[12,1024,1024]{2,1,0:T(8,128)}) fusion(f32[12,1024]{1,0:T(8,128)} %log_add_fusion, f32[12,1024,1024]{2,1,0:T(8,128)} %broadcast_multiply_fusion, f32[1024,1024]{1,0:T(8,128)} %broadcast_multiply_fusion.2, pred[1024,1024]{1,0:T(8,128)(4,1)} %compare_and_fusion.1, bf16[1024,12,64]{0,2,1:T(8,128)(2,1)} %bitcast.112, ...), kind=kOutput, calls=%fused_computation.1 | convolution fusion | flops 1686097920 | bytes 109150208 | tf_op jit(solution)/shard_map/ihd,jhd->hij/dot_general | solution.py:78
  337.5 54.2 %fusion.43 = (f32[1024,1024]{1,0:T(8,128)S(1)}, f32[12,1024,1024]{2,1,0:T(8,128)}) fusion(f32[12,1024,1024]{2,1,0:T(8,128)} %get-tuple-element.74, f32[12,1024]{1,0:T(8,128)} %get-tuple-element.73, f32[12,1024]{1,0:T(8,128)} %log_add_fusion, f32[12,1024,1024]{2,1,0:T(8,128)} %broadcast_multiply_fusion, f32[1024,1024]{1,0:T(8,128)} %broadcast_multiply_fusion.2, ...), kind=kLoop, calls=%fused_computation.122 | loop fusion | flops 87031808 | bytes 160530432 | tf_op jit(solution)/shard_map/reduce_sum | solution.py:83
  403.9 4.4 copy.101
  408.3 24.9 %slice.126 = bf16[11,1024,1024]{2,1,0:T(8,128)(2,1)} slice(f32[12,1024,1024]{2,1,0:T(8,128)} %get-tuple-element.58), slice={[1:12], [0:1024], [0:1024]} | slice | bytes 46137344 | tf_op jit(solution)/shard_map/slice | solution.py:86
  433.3 7.3 fusion.14
  441.9 10.9 %multiply_convert_fusion.1 = bf16[12,64,1024]{2,1,0:T(8,128)(2,1)} fusion(bf16[1024,12,64]{0,2,1:T(8,128)(2,1)S(1)} %bitcast.103, bf16[11,1024,1024]{2,1,0:T(8,128)(2,1)} %slice.126, bf16[1,1024,1024]{2,1,0:T(8,128)(2,1)S(1)} %fusion.14), kind=kOutput, calls=%fused_computation.60 | convolution fusion | flops 1624768512 | bytes 28311552 | tf_op jit(solution)/shard_map/hij,ihd->jhd/dot_general | solution.py:89
  452.8 14.9 %convert_reduce_fusion.4 = (f32[12,64]{1,0:T(8,128)}, bf16[12,64,1024]{2,1,0:T(8,128)(2,1)}) fusion(bf16[1024,12,64]{0,2,1:T(8,128)(2,1)} %bitcast.101, bf16[11,1024,1024]{2,1,0:T(8,128)(2,1)} %slice.126, bf16[1,1024,1024]{2,1,0:T(8,128)(2,1)} %copy-done.18), kind=kOutput, calls=%fused_computation.57 | convolution fusion | flops 1626340608 | bytes 28314624 | tf_op jit(solution)/shard_map/hij,jhd->ihd/dot_general | solution.py:88
  467.7 9.1 %convolution_convert_fusion.2 = bf16[768,2304]{1,0:T(8,128)(2,1)} fusion(bf16[1024,768]{0,1:T(8,128)(2,1)} %bitcast.118, bf16[1024,768]{0,1:T(8,128)(2,1)} %bitcast.120, bf16[1024,768]{0,1:T(8,128)(2,1)} %bitcast.124, f32[1024,768]{0,1:T(8,128)} %copy.108, f32[768]{0:T(1024)S(1)} %copy-done.40, f32[768]{0:T(1024)S(1)} %copy-done.29, ...), kind=kOutput, calls=%fused_computation.31 | convolution fusion | flops 3643736064 | bytes 11417600 | tf_op jit(solution)/shard_map/dot_general | solution.py:24
  477.5 12.2 %fusion.29 = bf16[1,1024,768]{1,2,0:T(8,128)(2,1)} fusion(f32[768]{0:T(1024)S(1)} %copy-done.41, f32[1024,768]{0,1:T(8,128)} %copy-done.4, bf16[3072,768]{1,0:T(8,128)(2,1)} %param.30, f32[1024,3072]{1,0:T(8,128)} %copy-done.12, f32[3072]{0:T(1024)} %param.29), kind=kOutput, calls=%fused_computation.85 | convolution fusion | flops 4865654784 | bytes 22035456 | tf_op jit(solution)/shard_map/dot_general | solution.py:24
  489.7 8.6 %copy.95 = bf16[1,1024,768]{2,0,1:T(2,128)(2,1)} copy(bf16[1,1024,768]{1,2,0:T(8,128)(2,1)} %fusion.29) | data formatting | bytes 3145728 | tf_op jit(solution)/shard_map/stack | solution.py:171
  498.8 12.4 %reduce.13 = bf16[1024,768]{1,0:T(8,128)(2,1)} reduce(bf16[1024,1,768]{2,1,0:T(2,128)(2,1)} %bitcast.96, bf16[]{:T(256)} %broadcast.204), dimensions={1}, to_apply=%bitcast.68.reduce_sub_computation | reduce | bytes 3145730
  511.2 3.7 reshape.272
  515.0 4.5 all-to-all-start.1
  520.9 8.6 %fusion.46 = (f32[768]{0:T(1024)}, f32[1024,768]{1,0:T(8,128)}) fusion(bf16[768,2304]{1,0:T(8,128)(2,1)S(1)} %copy-done, bf16[1024,768]{0,1:T(8,128)(2,1)} %bitcast.119, bf16[1024,768]{0,1:T(8,128)(2,1)} %bitcast.121, bf16[1024,768]{0,1:T(8,128)(2,1)} %bitcast.125), kind=kOutput, calls=%fused_computation.125 | convolution fusion | flops 3638820096 | bytes 11406336 | tf_op jit(solution)/shard_map/dot_general | solution.py:24
  533.0 4.1 multiply_reduce_fusion.2
  537.9 4.0 fusion.28
  541.9 8.6 %copy.103 = bf16[1,1024,768]{2,0,1:T(2,128)(2,1)} copy(bf16[1,1024,768]{1,2,0:T(8,128)(2,1)} %fusion.28) | data formatting | bytes 3145728 | tf_op jit(solution)/shard_map/convert_element_type | solution.py:176
  550.5 12.4 %reduce.14 = bf16[1024,768]{1,0:T(8,128)(2,1)} reduce(bf16[1024,1,768]{2,1,0:T(2,128)(2,1)} %bitcast.97, bf16[]{:T(256)} %broadcast.204), dimensions={1}, to_apply=%bitcast.66.reduce_sub_computation | reduce | bytes 3145730
  562.9 3.9 reshape.270
  566.8 4.4 all-to-all-start.3
  585.4 43.0 %psum.36 = f32[9216]{0:T(1024)} all-reduce(f32[9216]{0:T(1024)} %constant_dynamic-update-slice_fusion), channel_id=1, replica_groups=mesh['rows'=4,'cols'=8] {'rows','cols'}, use_global_device_ids=true, to_apply=%region_26.27 | all-reduce | flops 9216 | bytes 73728 | tf_op jit(solution)/shard_map/psum | solution.py:148
  631.1 6.4 reshape.273
  641.0 6.3 reshape.271
  647.3 3.8 copy.111
  651.1 85.2 %all-reduce.3.cloned.1.call-done = (bf16[768,2304]{1,0:T(8,128)(2,1)}, bf16[768,768]{1,0:T(8,128)(2,1)}, bf16[768,3072]{1,0:T(8,128)(2,1)}, bf16[3072,768]{1,0:T(8,128)(2,1)}) async-done(((bf16[768,2304]{1,0:T(8,128)(2,1)}, bf16[768,768]{1,0:T(8,128)(2,1)}, bf16[768,3072]{1,0:T(8,128)(2,1)}, bf16[3072,768]{1,0:T(8,128)(2,1)}), (bf16[768,2304]{1,0:T(8,128)(2,1)}, bf16[768,768]{1,0:T(8,128)(2,1)}, ...) | async-done | bytes 14155792 | tf_op jit(solution)/shard_map/psum | solution.py:147
  739.2 4.1 convert_element_type.158
  743.8 5.0 convert_element_type.167
  748.8 4.5 convert_element_type.169
  (158 shorter events, 92.0 us)
Async XLA Ops:
  7.2 57.6 %copy-start = (bf16[768,2304]{1,0:T(8,128)(2,1)S(1)}, bf16[768,2304]{1,0:T(8,128)(2,1)}, u32[]{:S(2)}) copy-start(bf16[768,2304]{1,0:T(8,128)(2,1)} %param.19) | copy-start | bytes 10616836
  7.2 26.6 %all-to-all-start = ((bf16[8,128,768]{2,1,0:T(8,128)(2,1)}), bf16[8,128,768]{2,1,0:T(8,128)(2,1)}, u32[]{:S(2)}, u32[]{:S(2)}) async-start(bf16[8,128,768]{2,1,0:T(8,128)(2,1)} %param.16), calls=%async_computation | async-start | bytes 3145728 | tf_op jit(solution)/shard_map/all_to_all | solution.py:15
  33.8 25.3 %all-to-all-start.2 = ((bf16[8,128,768]{2,1,0:T(8,128)(2,1)}), bf16[8,128,768]{2,1,0:T(8,128)(2,1)}, u32[]{:S(2)}, u32[]{:S(2)}) async-start(bf16[8,128,768]{2,1,0:T(8,128)(2,1)} %param.18), calls=%async_computation.2 | async-start | bytes 3145728 | tf_op jit(solution)/shard_map/all_to_all | solution.py:15
  38.1 698.2 %all-reduce.3.cloned.1.call-start = ((), (), s32[]{:S(2)}) async-start(), calls=%async_computation.4 | async-start | bytes 28311552 | tf_op jit(solution)/shard_map/psum | solution.py:147
  39.5 87.2 %copy-start.21 = (s32[1,1024]{1,0:T(1,128)}, s32[1,1024]{1,0:T(1,128)S(1)}, u32[]{:S(2)}) copy-start(s32[1,1024]{1,0:T(1,128)S(1)} %constant_dynamic-slice_fusion) | copy-start | bytes 12292
  42.8 21.9 %copy-start.24 = (f32[1024]{0:T(1024)}, f32[1024]{0:T(1024)S(1)}, u32[]{:S(2)}) copy-start(f32[1024]{0:T(1024)S(1)} %get-tuple-element.69) | copy-start | bytes 12292
  44.8 19.9 %copy-start.28 = (f32[768]{0:T(1024)S(1)}, f32[768]{0:T(1024)}, u32[]{:S(2)}) copy-start(f32[768]{0:T(1024)} %param.24) | copy-start | bytes 9220
  44.9 26.1 %copy-start.26 = (f32[1024]{0:T(1024)}, f32[1024]{0:T(1024)S(1)}, u32[]{:S(2)}) copy-start(f32[1024]{0:T(1024)S(1)} %rsqrt_bitcast_fusion) | copy-start | bytes 12292
  64.8 7.5 copy-start.35
  64.8 7.5 copy-start.36
  82.3 21.0 %copy-start.30 = (pred[1024]{0:T(1024)(128)(4,1)S(1)}, pred[1024]{0:T(1024)(128)(4,1)}, u32[]{:S(2)}) copy-start(pred[1024]{0:T(1024)(128)(4,1)} %add_not_fusion) | copy-start | bytes 3076
  126.7 4.9 copy-start.2
  179.4 20.8 %copy-start.39 = (f32[768]{0:T(1024)S(1)}, f32[768]{0:T(1024)}, u32[]{:S(2)}) copy-start(f32[768]{0:T(1024)} %param.23) | copy-start | bytes 9220
  200.2 5.0 slice-start
  200.2 4.9 slice-start.1
  200.2 4.9 copy-start.20
  200.2 4.9 copy-start.23
  204.7 45.8 %copy-start.4 = (f32[1024,768]{0,1:T(8,128)}, f32[1024,768]{0,1:T(8,128)S(1)}, u32[]{:S(2)}) copy-start(f32[1024,768]{0,1:T(8,128)S(1)} %get-tuple-element.72) | copy-start | bytes 9437188
  205.2 5.6 copy-start.38
  210.8 12.1 %copy-start.12 = (f32[1024,3072]{1,0:T(8,128)}, f32[1024,3072]{1,0:T(8,128)S(1)}, u32[]{:S(2)}) copy-start(f32[1024,3072]{1,0:T(8,128)S(1)} %fusion.42) | copy-start | bytes 37748740
  240.0 10.5 %copy-start.43 = (bf16[1024,3072]{1,0:T(8,128)(2,1)S(1)}, bf16[1024,3072]{1,0:T(8,128)(2,1)}, u32[]{:S(2)}) copy-start(bf16[1024,3072]{1,0:T(8,128)(2,1)} %get-tuple-element.84) | copy-start | bytes 18874372
  261.1 4.6 copy-start.5
  261.1 4.7 copy-start.8
  265.8 3.5 copy-start.42
  269.4 3.8 copy-start.13
  269.4 2.4 copy-start.37
  271.8 2.6 copy-start.1
  271.8 2.8 copy-start.3
  271.8 2.8 copy-start.19
  391.7 2.2 copy-start.6
  408.3 24.9 %copy-start.22 = (s32[1,1024]{1,0:T(1,128)S(1)}, s32[1,1024]{1,0:T(1,128)}, u32[]{:S(2)}) copy-start(s32[1,1024]{1,0:T(1,128)} %copy-done.21) | copy-start | bytes 12292
  408.3 24.9 %copy-start.31 = (pred[1024]{0:T(1024)(128)(4,1)S(1)}, pred[1024]{0:T(1024)(128)(4,1)}, u32[]{:S(2)}) copy-start(pred[1024]{0:T(1024)(128)(4,1)} %add_not_fusion) | copy-start | bytes 3076
  433.3 8.7 %copy-start.14 = (bf16[1024,768]{0,1:T(8,128)(2,1)S(1)}, bf16[1024,768]{0,1:T(8,128)(2,1)}, u32[]{:S(2)}) copy-start(bf16[1024,768]{0,1:T(8,128)(2,1)} %copy.90) | copy-start | bytes 4718596
  452.8 14.9 %copy-start.25 = (f32[1024]{0:T(1024)S(1)}, f32[1024]{0:T(1024)}, u32[]{:S(2)}) copy-start(f32[1024]{0:T(1024)} %copy-done.24) | copy-start | bytes 12292
  452.8 14.9 %copy-start.27 = (f32[1024]{0:T(1024)S(1)}, f32[1024]{0:T(1024)}, u32[]{:S(2)}) copy-start(f32[1024]{0:T(1024)} %copy-done.26) | copy-start | bytes 12292
  452.8 14.9 %copy-start.29 = (f32[768]{0:T(1024)S(1)}, f32[768]{0:T(1024)}, u32[]{:S(2)}) copy-start(f32[768]{0:T(1024)} %param.24) | copy-start | bytes 9220
  452.8 14.9 %copy-start.40 = (f32[768]{0:T(1024)S(1)}, f32[768]{0:T(1024)}, u32[]{:S(2)}) copy-start(f32[768]{0:T(1024)} %param.25) | copy-start | bytes 9220
  515.0 51.8 %all-to-all-start.1 = ((bf16[8,2,49152]{2,1,0:T(2,128)(2,1)}), bf16[8,2,49152]{2,1,0:T(2,128)(2,1)}, u32[]{:S(2)}, u32[]{:S(2)}) async-start(bf16[8,2,49152]{2,1,0:T(2,128)(2,1)} %reshape.272), calls=%async_computation.1 | async-start | bytes 3145728 | tf_op jit(solution)/shard_map/all_to_all | solution.py:19
  533.0 4.1 copy-start.7
  533.0 4.8 copy-start.9
  562.9 8.3 %copy-start.34 = (f32[768]{0:T(1024)S(1)}, f32[768]{0:T(1024)}, u32[]{:S(2)}) copy-start(f32[768]{0:T(1024)} %reduce_sum.196) | copy-start | bytes 9220
  562.9 11.7 %copy-start.33 = (f32[768]{0:T(1024)S(1)}, f32[768]{0:T(1024)}, u32[]{:S(2)}) copy-start(f32[768]{0:T(1024)} %get-tuple-element.55) | copy-start | bytes 9220
  562.9 15.6 %copy-start.32 = (f32[768]{0:T(1024)S(1)}, f32[768]{0:T(1024)}, u32[]{:S(2)}) copy-start(f32[768]{0:T(1024)} %get-tuple-element.45) | copy-start | bytes 9220
  566.8 74.2 %all-to-all-start.3 = ((bf16[8,2,49152]{2,1,0:T(2,128)(2,1)}), bf16[8,2,49152]{2,1,0:T(2,128)(2,1)}, u32[]{:S(2)}, u32[]{:S(2)}) async-start(bf16[8,2,49152]{2,1,0:T(2,128)(2,1)} %reshape.270), calls=%async_computation.3 | async-start | bytes 3145728 | tf_op jit(solution)/shard_map/all_to_all | solution.py:19
  736.2 3.0 copy-start.16
  739.2 4.5 copy-start.15
  739.2 9.6 %slice-start.2 = ((s8[4718592]{0:T(1024)(128)(4,1)}), s8[4194304]{0:T(1024)(128)(4,1)S(1)}, s32[]{:S(2)}) async-start(s8[4718592]{0:T(1024)(128)(4,1)} %bitcast.108), calls=%async_computation.7 | async-start | bytes 8388608
  743.8 5.1 slice-start.3
  (5 other events, 7.2 us)
Sparse Core Ops, SparseCore 0:
  476.9 259.2 all-reduce.2
